TPU v7x, 128 devices: a whole 4x4x4 slice. The times are simulated.
128 devices in a mesh: freq: 8 (over x, y_lo), mat: 16 (over z, y_hi, core).
Axes of the slice: x: 4, y: 4 (y_hi: 2, y_lo: 2; y = y_hi * 2 + y_lo), z: 4, core: 2. Of those that a mesh axis runs over, the one named last changes fastest.
Arguments:
- traces: bfloat16 [2048, 64, 4096], P('freq', None, 'mat'), may hold values from -6 to 6
- reflection: bfloat16 [16, 2, 4096, 4096], P('freq', None, 'mat'), may hold values from -0.0625 to 0.0625
- onset: int32 [64, 4096], P(None, 'mat'), may hold values from 512 to 2047
Outputs:
- windowed: bfloat16 [2048, 64, 4096], P('freq', None, 'mat')
Inputs may be any that keep to these rules, and one draw needn't show every extreme that they name: onset sample of the direct arrival for each focal point and receiver.
All inputs are finite; a program needn't handle non-finite values.
Results may differ from a plain program's by a relative error of at most 0.0069.
Values may be sent and summed in bfloat16 or wider, within the bound.
A program may use at most 128 MiB of HBM per device.

v0:
```python
import math
import jax
import jax.numpy as jnp
from jax import lax
from jax.sharding import PartitionSpec as P


def forward_table(
    base_band, first_band, band_count, earliest_sample_time, sample_time_count, sampling_interval
):
    angular_freq_list = base_band + first_band + jnp.arange(band_count, dtype=jnp.int32)
    sample_moments = earliest_sample_time + jnp.arange(sample_time_count, dtype=jnp.int32)
    phase_angles = (
        angular_freq_list[:, None] * sample_moments[None, :] % sampling_interval
    ).astype(jnp.float32) * (2.0 * math.pi / sampling_interval)
    factor = 1.0 / math.sqrt(sampling_interval)
    table = jnp.stack([jnp.cos(phase_angles) * factor, -jnp.sin(phase_angles) * factor], axis=1)
    return table.reshape(2 * band_count, sample_time_count).astype(jnp.bfloat16)


def inverse_table(
    base_band,
    first_band,
    band_count,
    earliest_sample_time,
    sample_time_count,
    sampling_interval,
    bands_total,
):
    angular_freq_list = base_band + first_band + jnp.arange(band_count, dtype=jnp.int32)
    sample_moments = earliest_sample_time + jnp.arange(sample_time_count, dtype=jnp.int32)
    phase_angles = (
        sample_moments[:, None] * angular_freq_list[None, :] % sampling_interval
    ).astype(jnp.float32) * (2.0 * math.pi / sampling_interval)
    factor = 1.0 / math.sqrt(bands_total)
    table = jnp.stack([jnp.cos(phase_angles) * factor, -jnp.sin(phase_angles) * factor], axis=2)
    return table.reshape(sample_time_count, 2 * band_count).astype(jnp.bfloat16)


def accumulate(reflection, panels):
    return jnp.einsum("kcpw,kdrw->kcpdr", panels, reflection, preferred_element_type=jnp.float32)


def on_device(traces, reflection, onset):
    temporal_rows, focal_count, recv_rows = traces.shape
    freq_devices = lax.axis_size("freq")
    sampling_interval = temporal_rows * freq_devices
    per_device = reflection.shape[0]
    bands_total = per_device * freq_devices
    base_band = sampling_interval // 16
    earliest_sample_time = lax.axis_index("freq") * temporal_rows
    earliest = lax.axis_index("freq") * temporal_rows
    forward = forward_table(base_band, 0, bands_total, earliest, temporal_rows, sampling_interval)
    partial = jnp.dot(
        forward, traces.reshape(temporal_rows, -1), preferred_element_type=jnp.float32
    )
    partial = partial.astype(jnp.bfloat16).reshape(
        freq_devices, per_device, 2, focal_count, recv_rows
    )
    parts = lax.all_to_all(partial, "freq", split_axis=0, concat_axis=0, tiled=True)
    spectra = jnp.sum(parts.astype(jnp.float32), axis=0).astype(jnp.bfloat16)
    products = accumulate(reflection, lax.all_gather(spectra, "mat", axis=3, tiled=True))
    real_part = products[:, 0, :, 0] - products[:, 1, :, 1]
    imag_part = products[:, 1, :, 0] + products[:, 0, :, 1]
    response = jnp.stack([real_part, imag_part], axis=1).astype(jnp.bfloat16)
    pieces = lax.all_gather(response, "freq", axis=0, tiled=True)
    piece_bands = pieces.shape[0]
    table = inverse_table(
        base_band,
        jnp.int32(0),
        piece_bands,
        earliest_sample_time,
        temporal_rows,
        sampling_interval,
        bands_total,
    )
    wavelet_trace = jnp.dot(
        table, pieces.reshape(2 * piece_bands, -1), preferred_element_type=jnp.float32
    )
    wavelet_trace = wavelet_trace.reshape(temporal_rows, focal_count, recv_rows)
    sample_moments = earliest_sample_time + jnp.arange(temporal_rows, dtype=jnp.int32)
    return jnp.where(sample_moments[:, None, None] < onset[None], wavelet_trace, 0.0).astype(
        jnp.bfloat16
    )


def solution(mesh):
    placed = (P("freq", None, "mat"), P("freq", None, "mat", None), P(None, "mat"))
    return jax.shard_map(
        on_device, mesh=mesh, in_specs=placed, out_specs=P("freq", None, "mat"), check_vma=False
    )
```

profile of v0, /device:TPU:0, one launch (start us, length us, event | category | flops | bytes accessed | tf_op | source)
XLA Modules:
  0.0 166.1 jit_solution(9028758283541389684)
XLA Ops:
  6.5 0.0 all-gather.3.cloned.1.call-start
  6.5 0.2 multiply_convert_fusion.1
  6.8 15.4 %copy.29 = bf16[32,8,64,256]{3,1,2,0:T(8,128)(2,1)} copy(bf16[32,8,64,256]{3,2,1,0:T(8,128)(2,1)} %bitcast.51) | data formatting | bytes 16777216
  22.2 4.9 %convolution_convert_fusion = bf16[32,16384]{1,0:T(8,128)(2,1)S(1)} fusion(bf16[32,256]{1,0:T(8,128)(2,1)S(1)} %convert_element_type.60, bf16[256,16384]{1,0:T(8,128)(2,1)} %bitcast.50), kind=kOutput, calls=%fused_computation | convolution fusion | flops 268959744 | bytes 9453568 | tf_op jit(solution)/shard_map/dot_general | solution.py:54
  27.1 0.2 copy.30
  27.3 0.0 copy-start
  27.4 20.7 %all_to_all.5 = bf16[8,2,2,64,256]{4,3,2,1,0:T(8,128)(2,1)S(1)} all-to-all(bf16[8,2,2,64,256]{4,3,2,1,0:T(8,128)(2,1)S(1)} %bitcast.53), channel_id=1, replica_groups=mesh['freq'=8,'mat'=16] {'freq'}, dimensions={0} | all-to-all | bytes 2097152 | tf_op jit(solution)/shard_map/all_to_all | solution.py:60
  48.0 0.8 reduce_sum.12
  48.8 0.0 all-gather.3.cloned.1.call-update
  48.9 0.2 all-gather.5.cloned.1.call-start
  49.1 47.8 %all-gather.3.cloned.1.call-done = bf16[2,2,64,4096]{3,2,1,0:T(8,128)(2,1)} async-done(((bf16[2,2,64,256]{3,2,1,0:T(8,128)(2,1)}), bf16[2,2,64,4096]{3,2,1,0:T(8,128)(2,1)}) %all-gather.3.cloned.1.call-update) | async-done | bytes 2097168 | tf_op jit(solution)/shard_map/all_gather | solution.py:62
  96.9 6.9 %fusion = f32[2,2,64,2,256]{4,2,3,1,0:T(8,128)S(1)} fusion(bf16[2,2,256,4096]{3,2,1,0:T(8,128)(2,1)} %param.4, bf16[2,2,64,4096]{3,2,1,0:T(8,128)(2,1)} %all-gather.3.cloned.1.call-done), kind=kOutput, calls=%fused_computation.2 | convolution fusion | flops 1073741824 | bytes 11010048 | tf_op jit(solution)/shard_map/kcpw,kdrw->kcpdr/dot_general | solution.py:41
  103.9 0.7 pad_maximum_fusion
  104.5 0.0 all-gather.5.cloned.1.call-update
  104.6 0.2 multiply_convert_fusion.3
  104.8 37.0 %all-gather.5.cloned.1.call-done = bf16[16,2,64,256]{3,2,0,1:T(8,128)(2,1)} async-done(((bf16[2,2,64,256]{3,2,0,1:T(8,128)(2,1)}), bf16[16,2,64,256]{3,2,0,1:T(8,128)(2,1)}) %all-gather.5.cloned.1.call-update) | async-done | bytes 1048592 | tf_op jit(solution)/shard_map/all_gather | solution.py:66
  141.8 1.3 copy.21
  143.0 0.0 copy-done
  143.1 4.7 %select_convert_fusion = bf16[256,64,256]{2,0,1:T(8,128)(2,1)} fusion(bf16[256,32,1]{0,1,2:T(8,128)(2,1)S(1)} %reshape.357, s32[64,256]{1,0:T(8,128)S(1)} %copy-done, s32[256]{0:T(256)S(1)} %iota_add_fusion, bf16[4,8,64,256]{3,2,1,0:T(8,128)(2,1)S(1)} %bitcast.54), kind=kOutput, calls=%fused_computation.1 | convolution fusion | flops 281018368 | bytes 9520128 | tf_op jit(solution)/shard_map/dot_general | solution.py:77
  147.7 11.5 %copy.23 = bf16[256,64,256]{2,1,0:T(8,128)(2,1)} copy(bf16[256,64,256]{2,0,1:T(8,128)(2,1)} %select_convert_fusion) | data formatting | bytes 16777216 | tf_op jit(solution)/shard_map/convert_element_type | solution.py:82
  (10 shorter events, 0.1 us)
Async XLA Ops:
  6.5 90.3 %all-gather.3.cloned.1.call-start = ((), (), s32[]{:S(2)}) async-start(), calls=%async_computation.1 | async-start | bytes 2228224 | tf_op jit(solution)/shard_map/all_gather | solution.py:62
  27.3 115.7 %copy-start = (s32[64,256]{1,0:T(8,128)S(1)}, s32[64,256]{1,0:T(8,128)}, u32[]{:S(2)}) copy-start(s32[64,256]{1,0:T(8,128)} %param.5) | copy-start | bytes 196612
  48.9 92.9 %all-gather.5.cloned.1.call-start = ((), (), s32[]{:S(2)}) async-start(), calls=%async_computation.2 | async-start | bytes 1179648 | tf_op jit(solution)/shard_map/all_gather | solution.py:66
Sparse Core Ops, SparseCore 0:
  49.0 47.8 all-gather.2
  104.7 37.0 all-gather.4
where the time goes:
time: 166 us
  waiting for transfers between devices  84.8 us (51%)
  local copies, waits for them, and re-layouts  28.6 us (17%)
  blocking collectives  20.7 us (12%)
  matrix products  16.5 us (10%)
  between operations  13.5 us (8%)
  other arithmetic  1.84 us (1%)
    all_gather x1, waiting for transfers between devices, on_device(): lax.all_gather(spectra, 'mat', axis=3, tiled=True)  47.8 us
    all_gather x1, waiting for transfers between devices, on_device(): pieces = lax.all_gather(response, 'freq', axis=0, tiled=True)  37 us
    all_to_all x1, blocking collectives, on_device(): lax.all_to_all(partial, 'freq', split_axis=0, concat_axis=0, tiled=True)  20.7 us
    unnamed x4, local copies, waits for them, and re-layouts  15.7 us
    convert_element_type x1, local copies, waits for them, and re-layouts, on_device(): jnp.where(sample_moments[:, None, None] < onset[None], wavelet_trace, 0.0)  11.5 us
    dot_general x1, matrix products, accumulate(): jnp.einsum('kcpw,kdrw->kcpdr', panels, reflection, preferred_element_type...  6.94 us
    dot_general x1, matrix products, on_device(): jnp.dot(forward, traces.reshape(temporal_rows, -1), preferred_element_typ...  4.92 us
    dot_general x1, matrix products, on_device(): jnp.dot(table, pieces.reshape(2 * piece_bands, -1), preferred_element_typ...  4.66 us
  transfers between devices with their start and end apart: 2, of which 2 were waited for; matrix products, arithmetic and copies ran while one was open for 0% of the time, Pallas kernels for 0%

commit v1 on v0

--- a/solution.py
+++ b/solution.py
@@ -59,7 +59,12 @@
     )
     parts = lax.all_to_all(partial, "freq", split_axis=0, concat_axis=0, tiled=True)
     spectra = jnp.sum(parts.astype(jnp.float32), axis=0).astype(jnp.bfloat16)
-    products = accumulate(reflection, lax.all_gather(spectra, "mat", axis=3, tiled=True))
+    products = accumulate(
+        reflection,
+        jnp.concatenate(
+            lax.all_to_all(jnp.stack([spectra] * lax.axis_size("mat")), "mat", 0, 0), axis=3
+        ),
+    )
     real_part = products[:, 0, :, 0] - products[:, 1, :, 1]
     imag_part = products[:, 1, :, 0] + products[:, 0, :, 1]
     response = jnp.stack([real_part, imag_part], axis=1).astype(jnp.bfloat16)

time: 166 us -> 155 us (0.934)
  waiting for transfers between devices: 84.8 us -> 34.2 us
  blocking collectives: 20.7 us -> 57.3 us
  local copies, waits for them, and re-layouts: 28.6 us -> 32.4 us
    all_gather x1 -> x0, waiting for transfers between devices: 47.8 us -> none  [on_device(): lax.all_gather(spectra, 'mat', axis=3, tiled=True)]
    all_to_all x0 -> x1, blocking collectives: none -> 36.8 us  [on_device(): lax.all_to_all(jnp.stack([spectra] * lax.axis_size('mat')), 'mat', 0, 0)]
    reshape x0 -> x2, local copies, waits for them, and re-layouts: none -> 3.55 us  [on_device(): jnp.concatenate(lax.all_to_all(jnp.stack([spectra] * lax.axis_size('mat')...]
    all_gather x1, waiting for transfers between devices: 37 us -> 34.2 us  [on_device(): pieces = lax.all_gather(response, 'freq', axis=0, tiled=True)]
  transfers between devices with their start and end apart: 2 -> 1, of which waited for: 2 -> 1; matrix products, arithmetic and copies ran while one was open for 0% -> 0% of each run, Pallas kernels for 0% -> 0%
where the time goes in v1:
time: 155 us
  blocking collectives  57.3 us (37%)
  waiting for transfers between devices  34.2 us (22%)
  local copies, waits for them, and re-layouts  32.4 us (21%)
  matrix products  16.5 us (11%)
  between operations  13.5 us (9%)
    all_to_all x1, blocking collectives, on_device(): lax.all_to_all(jnp.stack([spectra] * lax.axis_size('mat')), 'mat', 0, 0)  36.8 us
    all_gather x1, waiting for transfers between devices, on_device(): pieces = lax.all_gather(response, 'freq', axis=0, tiled=True)  34.2 us
    all_to_all x1, blocking collectives, on_device(): lax.all_to_all(partial, 'freq', split_axis=0, concat_axis=0, tiled=True)  20.5 us
    unnamed x4, local copies, waits for them, and re-layouts  15.7 us
    convert_element_type x1, local copies, waits for them, and re-layouts, on_device(): jnp.where(sample_moments[:, None, None] < onset[None], wavelet_trace, 0.0)  11.5 us
    dot_general x1, matrix products, accumulate(): jnp.einsum('kcpw,kdrw->kcpdr', panels, reflection, preferred_element_type...  6.94 us
    dot_general x1, matrix products, on_device(): jnp.dot(forward, traces.reshape(temporal_rows, -1), preferred_element_typ...  4.92 us
    dot_general x1, matrix products, on_device(): jnp.dot(table, pieces.reshape(2 * piece_bands, -1), preferred_element_typ...  4.66 us
  transfers between devices with their start and end apart: 1, of which 1 were waited for; matrix products, arithmetic and copies ran while one was open for 0% of the time, Pallas kernels for 0%

profile of v1, /device:TPU:0, one launch (start us, length us, event | category | flops | bytes accessed | tf_op | source)
XLA Modules:
  0.0 155.1 jit_solution(15277624855126942181)
XLA Ops:
  6.5 0.0 all-gather.2.cloned.1.call-start
  6.5 0.2 multiply_convert_fusion.1
  6.8 15.4 %copy.37 = bf16[32,8,64,256]{3,1,2,0:T(8,128)(2,1)} copy(bf16[32,8,64,256]{3,2,1,0:T(8,128)(2,1)} %bitcast.52) | data formatting | bytes 16777216
  22.2 4.9 %convolution_convert_fusion = bf16[32,16384]{1,0:T(8,128)(2,1)S(1)} fusion(bf16[32,256]{1,0:T(8,128)(2,1)S(1)} %convert_element_type.60, bf16[256,16384]{1,0:T(8,128)(2,1)} %bitcast.51), kind=kOutput, calls=%fused_computation | convolution fusion | flops 268959744 | bytes 9453568 | tf_op jit(solution)/shard_map/dot_general | solution.py:54
  27.1 0.2 copy.38
  27.3 20.5 %all_to_all.10 = bf16[8,2,2,64,256]{4,3,2,1,0:T(8,128)(2,1)S(1)} all-to-all(bf16[8,2,2,64,256]{4,3,2,1,0:T(8,128)(2,1)S(1)} %bitcast.55), channel_id=1, replica_groups=mesh['freq'=8,'mat'=16] {'freq'}, dimensions={0} | all-to-all | bytes 2097152 | tf_op jit(solution)/shard_map/all_to_all | solution.py:60
  47.9 0.1 reduce_sum.12
  48.0 0.2 stack.13
  48.3 36.8 %all_to_all.11 = bf16[16,2,2,64,256]{4,3,2,1,0:T(8,128)(2,1)S(1)} all-to-all(bf16[16,2,2,64,256]{4,3,2,1,0:T(8,128)(2,1)S(1)} %stack.13), channel_id=1, replica_groups=mesh['freq'=8,'mat'=16] {'mat'}, dimensions={0} | all-to-all | bytes 4194304 | tf_op jit(solution)/shard_map/all_to_all | solution.py:65
  85.1 1.2 copy.26
  86.3 0.0 copy-start
  86.3 2.3 %reshape.365 = bf16[2,2,64,4096,1]{3,2,1,0,4:T(8,128)(2,1)} reshape(bf16[2,2,64,16,256]{4,3,2,1,0:T(8,128)(2,1)S(1)} %copy.26) | data formatting | bytes 4194304 | tf_op jit(solution)/shard_map/reshape | solution.py:64
  88.6 6.9 %fusion = f32[2,2,64,2,256]{4,2,3,1,0:T(8,128)S(1)} fusion(bf16[2,2,256,4096]{3,2,1,0:T(8,128)(2,1)} %param.4, bf16[2,2,64,4096,1]{3,2,1,0,4:T(8,128)(2,1)} %reshape.365), kind=kOutput, calls=%fused_computation.2 | convolution fusion | flops 1073741824 | bytes 11010048 | tf_op jit(solution)/shard_map/kcpw,kdrw->kcpdr/dot_general | solution.py:41
  95.6 0.7 pad_maximum_fusion
  96.3 0.0 all-gather.2.cloned.1.call-update
  96.3 0.2 multiply_convert_fusion.3
  96.5 34.2 %all-gather.2.cloned.1.call-done = bf16[16,2,64,256]{3,2,0,1:T(8,128)(2,1)} async-done(((bf16[2,2,64,256]{3,2,0,1:T(8,128)(2,1)}), bf16[16,2,64,256]{3,2,0,1:T(8,128)(2,1)}) %all-gather.2.cloned.1.call-update) | async-done | bytes 1048592 | tf_op jit(solution)/shard_map/all_gather | solution.py:71
  130.7 1.3 copy.29
  132.0 0.0 copy-done
  132.0 4.7 %select_convert_fusion = bf16[256,64,256]{2,0,1:T(8,128)(2,1)} fusion(bf16[256,32,1]{0,1,2:T(8,128)(2,1)S(1)} %reshape.367, s32[64,256]{1,0:T(8,128)S(1)} %copy-done, s32[256]{0:T(256)S(1)} %iota_add_fusion, bf16[4,8,64,256]{3,2,1,0:T(8,128)(2,1)S(1)} %bitcast.56), kind=kOutput, calls=%fused_computation.1 | convolution fusion | flops 281018368 | bytes 9520128 | tf_op jit(solution)/shard_map/dot_general | solution.py:82
  136.7 11.5 %copy.31 = bf16[256,64,256]{2,1,0:T(8,128)(2,1)} copy(bf16[256,64,256]{2,0,1:T(8,128)(2,1)} %select_convert_fusion) | data formatting | bytes 16777216 | tf_op jit(solution)/shard_map/convert_element_type | solution.py:87
  (10 shorter events, 0.1 us)
Async XLA Ops:
  6.5 124.2 %all-gather.2.cloned.1.call-start = ((), (), s32[]{:S(2)}) async-start(), calls=%async_computation.2 | async-start | bytes 1179648 | tf_op jit(solution)/shard_map/all_gather | solution.py:71
  86.3 45.7 %copy-start = (s32[64,256]{1,0:T(8,128)S(1)}, s32[64,256]{1,0:T(8,128)}, u32[]{:S(2)}) copy-start(s32[64,256]{1,0:T(8,128)} %param.5) | copy-start | bytes 196612
Sparse Core Ops, SparseCore 0:
  96.4 34.2 all-gather.1
